TPU v7x, 32 devices: a whole 2x2x4 slice. The times are simulated.
32 devices in a mesh: seq: 8 (over y, x, core), head: 4 (over z).
Axes of the slice: x: 2, y: 2, z: 4, core: 2. Of those that a mesh axis runs over, the one named last changes fastest.
Arguments:
- queries: bfloat16 [4096, 8192], P(('seq', 'head')), may hold values from -18 to 18
- keys: bfloat16 [4096, 1024], P(('seq', 'head')), may hold values from -18 to 18
- values: bfloat16 [4096, 1024], P(('seq', 'head')), may hold values from -6 to 6
- grad_out: bfloat16 [4096, 8192], P(('seq', 'head')), may hold values from -6 to 6
- starts: int32 [8], replicated, may hold values from 0 to 4095, as said below
- pattern: int32 [32, 5], replicated, may hold values from 0 to 1, as said below
Outputs:
- query_grads: bfloat16 [4096, 8192], P(('seq', 'head'))
- key_grads: bfloat16 [4096, 1024], P(('seq', 'head'))
- value_grads: bfloat16 [4096, 1024], P(('seq', 'head'))
Inputs may be any that keep to these rules, and one draw needn't show every extreme that they name: starts[0] is 0, the offsets rise strictly and the last is 4095; sequence i runs from starts[i] to the next offset (the last to the end). `pattern`: column 0 is all ones.
All inputs are finite; a program needn't handle non-finite values.
Results may differ from a plain program's by a relative error of at most 0.0074.
Values may be sent and summed in bfloat16 or wider, within the bound.
A program may use at most 192 MiB of HBM per device.

v0:
```python
import math

import jax
import jax.numpy as jnp
from jax import lax
from jax.sharding import PartitionSpec as P

KV_HEADS = 8
HEAD_DIM = 128
WINDOW = 512
BLOCK = 128


def from_behind(value, axis, by):
    devices = lax.axis_size(axis)
    pairs = [(i, i + by) for i in range(devices) if 0 <= i + by < devices]
    return lax.ppermute(value, axis, pairs)


def segment_of(positions, starts):
    return jnp.sum((starts[None, :] <= positions[:, None]).astype(jnp.int32), axis=1) - 1


def block_allowed(first_row, starts, pattern):
    query_pos = first_row + jnp.arange(WINDOW, dtype=jnp.int32)
    key_pos = first_row - WINDOW + jnp.arange(2 * WINDOW, dtype=jnp.int32)
    per_block = WINDOW // BLOCK
    pattern_rows = lax.dynamic_slice(
        pattern, (first_row // BLOCK, jnp.zeros((), jnp.int32)), (per_block, per_block + 1)
    )
    relative = (
        jnp.arange(per_block, dtype=jnp.int32)[:, None]
        - jnp.arange(2 * per_block, dtype=jnp.int32)[None, :]
        + per_block
    )
    matches = (
        jnp.arange(per_block + 1, dtype=jnp.int32)[None, None, :] == relative[:, :, None]
    ).astype(jnp.int32)
    chosen = jnp.sum(pattern_rows[:, None, :] * matches, axis=2)
    block_open = jnp.repeat(jnp.repeat(chosen, BLOCK, axis=0), BLOCK, axis=1) > 0
    query_col = query_pos[:, None]
    key_row = key_pos[None, :]
    same_seq = segment_of(query_pos, starts)[:, None] == segment_of(key_pos, starts)[None, :]
    return (
        (key_row <= query_col)
        & (query_col - key_row < WINDOW)
        & (key_row >= 0)
        & same_seq
        & block_open
    )


def block_grads(query_blk, key_blk, value_blk, grad_blk, allowed, kv_local, head_dim):
    count_rows = query_blk.shape[0]
    count_keys = key_blk.shape[0]
    query_heads = query_blk.reshape(count_rows, kv_local, -1, head_dim)
    grad_heads = grad_blk.reshape(count_rows, kv_local, -1, head_dim)
    key_heads = key_blk.reshape(count_keys, kv_local, head_dim)
    value_heads = value_blk.reshape(count_keys, kv_local, head_dim)
    score_scale = 1.0 / math.sqrt(head_dim)
    score = score_scale * jnp.einsum(
        "rkgd,nkd->kgrn", query_heads, key_heads, preferred_element_type=jnp.float32
    )
    mask = allowed[None, None]
    peak = jnp.max(jnp.where(mask, score, -1e30), axis=-1, keepdims=True)
    expo = jnp.exp(jnp.where(mask, score - peak, -1e30))
    probs = expo / jnp.sum(expo, axis=-1, keepdims=True)
    probs_low = probs.astype(jnp.bfloat16)
    value_grad = jnp.einsum(
        "kgrn,rkgd->nkd", probs_low, grad_heads, preferred_element_type=jnp.float32
    )
    prob_grad = jnp.einsum(
        "rkgd,nkd->kgrn", grad_heads, value_heads, preferred_element_type=jnp.float32
    )
    row_dot = jnp.sum(probs * prob_grad, axis=-1, keepdims=True)
    score_grad = (probs * (prob_grad - row_dot)).astype(jnp.bfloat16)
    query_grad = score_scale * jnp.einsum(
        "kgrn,nkd->rkgd", score_grad, key_heads, preferred_element_type=jnp.float32
    )
    key_grad = score_scale * jnp.einsum(
        "kgrn,rkgd->nkd", score_grad, query_heads, preferred_element_type=jnp.float32
    )
    return (
        query_grad.reshape(count_rows, -1),
        key_grad.reshape(count_keys, -1),
        value_grad.reshape(count_keys, -1),
    )


def regrouped_body(queries, keys, values, grad_out, starts, pattern):
    query_loc, key_loc, value_loc, grad_loc = (
        lax.all_to_all(queries, "head", split_axis=1, concat_axis=0, tiled=True),
        lax.all_to_all(keys, "head", split_axis=1, concat_axis=0, tiled=True),
        lax.all_to_all(values, "head", split_axis=1, concat_axis=0, tiled=True),
        lax.all_to_all(grad_out, "head", split_axis=1, concat_axis=0, tiled=True),
    )
    local_rows = key_loc.shape[0]
    rim_rows = from_behind(
        jnp.stack([key_loc[local_rows - WINDOW :], value_loc[local_rows - WINDOW :]]), "seq", 1
    )
    prior_keys = rim_rows[0]
    prior_values = rim_rows[1]
    kv_local = KV_HEADS // lax.axis_size("head")
    kv_width = key_loc.shape[1]
    key_ext = jnp.concatenate([prior_keys, key_loc], axis=0)
    value_ext = jnp.concatenate([prior_values, value_loc], axis=0)
    base_row = lax.axis_index("seq") * local_rows

    def step(carry, block_index):
        key_acc, value_acc = carry
        local_first = block_index * WINDOW
        allowed = block_allowed(base_row + local_first, starts, pattern)
        query_blk = lax.dynamic_slice_in_dim(query_loc, local_first, WINDOW, 0)
        grad_blk = lax.dynamic_slice_in_dim(grad_loc, local_first, WINDOW, 0)
        key_blk = lax.dynamic_slice_in_dim(key_ext, local_first, 2 * WINDOW, 0)
        value_blk = lax.dynamic_slice_in_dim(value_ext, local_first, 2 * WINDOW, 0)
        query_grad, key_grad, value_grad = block_grads(
            query_blk, key_blk, value_blk, grad_blk, allowed, kv_local, HEAD_DIM
        )
        key_acc = lax.dynamic_update_slice_in_dim(
            key_acc,
            lax.dynamic_slice_in_dim(key_acc, local_first, 2 * WINDOW, 0) + key_grad,
            local_first,
            0,
        )
        value_acc = lax.dynamic_update_slice_in_dim(
            value_acc,
            lax.dynamic_slice_in_dim(value_acc, local_first, 2 * WINDOW, 0) + value_grad,
            local_first,
            0,
        )
        return ((key_acc, value_acc), query_grad.astype(jnp.bfloat16))

    empty = jnp.zeros((WINDOW + local_rows, kv_width), jnp.float32)
    (key_acc, value_acc), query_parts = lax.scan(
        step, (empty, empty), jnp.arange(local_rows // WINDOW, dtype=jnp.int32)
    )
    returned = from_behind(jnp.stack([key_acc[:WINDOW], value_acc[:WINDOW]]), "seq", -1)
    own_keys = key_acc[WINDOW:].at[local_rows - WINDOW :].add(returned[0])
    own_values = value_acc[WINDOW:].at[local_rows - WINDOW :].add(returned[1])
    query_grads, key_grads, value_grads = (
        lax.all_to_all(
            query_parts.reshape(local_rows, -1), "head", split_axis=0, concat_axis=1, tiled=True
        ),
        lax.all_to_all(
            own_keys.astype(jnp.bfloat16), "head", split_axis=0, concat_axis=1, tiled=True
        ),
        lax.all_to_all(
            own_values.astype(jnp.bfloat16), "head", split_axis=0, concat_axis=1, tiled=True
        ),
    )
    return (query_grads, key_grads, value_grads)


def body(queries, keys, values, grad_out, starts, pattern):
    return regrouped_body(queries, keys, values, grad_out, starts, pattern)


def solution(mesh):
    in_specs = (
        P(("seq", "head"), None),
        P(("seq", "head"), None),
        P(("seq", "head"), None),
        P(("seq", "head"), None),
        P(),
        P(),
    )
    out_specs = (P(("seq", "head"), None), P(("seq", "head"), None), P(("seq", "head"), None))
    return jax.shard_map(body, mesh=mesh, in_specs=in_specs, out_specs=out_specs, check_vma=False)
```

profile of v0, /device:TPU:4, one launch (start us, length us, event | category | flops | bytes accessed | tf_op | source)
XLA Modules:
  0.0 337.6 jit_solution(3752999608414127778)
XLA Ops:
  0.7 1.8 copy.127
  2.5 4.9 %all-to-all-start = ((bf16[128,4,256]{0,2,1:T(8,128)(2,1)}), bf16[128,4,256]{0,2,1:T(8,128)(2,1)S(1)}, u32[]{:S(2)}, u32[]{:S(2)}) async-start(bf16[128,4,256]{0,2,1:T(8,128)(2,1)} %bitcast), calls=%async_computation | async-start | bytes 524288 | tf_op jit(solution)/shard_map/all_to_all | solution.py:93
  7.3 1.8 copy.129
  9.1 7.1 %all-to-all-done = bf16[128,4,256]{0,2,1:T(8,128)(2,1)S(1)} async-done(((bf16[128,4,256]{0,2,1:T(8,128)(2,1)}), bf16[128,4,256]{0,2,1:T(8,128)(2,1)S(1)}, u32[]{:S(2)}, u32[]{:S(2)}) %all-to-all-start) | async-done | bytes 262176 | tf_op jit(solution)/shard_map/all_to_all | solution.py:93
  16.2 3.4 %all-to-all-start.1 = ((bf16[128,4,256]{0,2,1:T(8,128)(2,1)}), bf16[128,4,256]{0,2,1:T(8,128)(2,1)S(1)}, u32[]{:S(2)}, u32[]{:S(2)}) async-start(bf16[128,4,256]{0,2,1:T(8,128)(2,1)} %bitcast.3), calls=%async_computation.1 | async-start | bytes 524288 | tf_op jit(solution)/shard_map/all_to_all | solution.py:94
  19.7 3.2 copy.176
  22.8 3.8 %all-to-all-done.1 = bf16[128,4,256]{0,2,1:T(8,128)(2,1)S(1)} async-done(((bf16[128,4,256]{0,2,1:T(8,128)(2,1)}), bf16[128,4,256]{0,2,1:T(8,128)(2,1)S(1)}, u32[]{:S(2)}, u32[]{:S(2)}) %all-to-all-start.1) | async-done | bytes 262176 | tf_op jit(solution)/shard_map/all_to_all | solution.py:94
  26.7 3.6 %all-to-all-start.2 = ((bf16[128,4,2048]{2,0,1:T(8,128)(2,1)}), bf16[128,4,2048]{2,0,1:T(8,128)(2,1)S(1)}, u32[]{:S(2)}, u32[]{:S(2)}) async-start(bf16[128,4,2048]{2,0,1:T(8,128)(2,1)} %bitcast.125), calls=%async_computation.2 | async-start | bytes 4194304 | tf_op jit(solution)/shard_map/all_to_all | solution.py:92
  30.3 3.2 copy.175
  33.4 42.3 %all-to-all-done.2 = bf16[128,4,2048]{2,0,1:T(8,128)(2,1)S(1)} async-done(((bf16[128,4,2048]{2,0,1:T(8,128)(2,1)}), bf16[128,4,2048]{2,0,1:T(8,128)(2,1)S(1)}, u32[]{:S(2)}, u32[]{:S(2)}) %all-to-all-start.2) | async-done | bytes 2097184 | tf_op jit(solution)/shard_map/all_to_all | solution.py:92
  75.7 4.4 %all-to-all-start.3 = ((bf16[128,4,2048]{2,0,1:T(8,128)(2,1)}), bf16[128,4,2048]{2,0,1:T(8,128)(2,1)}, u32[]{:S(2)}, u32[]{:S(2)}) async-start(bf16[128,4,2048]{2,0,1:T(8,128)(2,1)} %bitcast.123), calls=%async_computation.3 | async-start | bytes 4194304 | tf_op jit(solution)/shard_map/all_to_all | solution.py:95
  80.9 0.8 pad_maximum_fusion.1
  81.7 1.9 collective-permute-start
  83.7 1.8 fusion.18
  85.7 0.7 copy.140
  86.5 7.0 %collective-permute-done = bf16[2,512,256]{2,1,0:T(8,128)(2,1)} collective-permute-done((bf16[2,512,256]{2,1,0:T(8,128)(2,1)}, bf16[2,512,256]{2,1,0:T(8,128)(2,1)}, u32[]{:S(2)}, u32[]{:S(2)}) %collective-permute-start) | collective-permute-done | bytes 524320 | tf_op jit(solution)/shard_map/ppermute | solution.py:17
  93.4 1.1 fusion.40
  95.0 0.8 copy.139
  95.8 1.9 copy.171
  97.8 3.0 copy.147
  100.8 27.1 %all-to-all-done.3 = bf16[128,4,2048]{2,0,1:T(8,128)(2,1)} async-done(((bf16[128,4,2048]{2,0,1:T(8,128)(2,1)}), bf16[128,4,2048]{2,0,1:T(8,128)(2,1)}, u32[]{:S(2)}, u32[]{:S(2)}) %all-to-all-start.3) | async-done | bytes 2097184 | tf_op jit(solution)/shard_map/all_to_all | solution.py:95
  127.9 3.5 %copy.172 = bf16[64,8,16,128]{3,2,1,0:T(8,128)(2,1)} copy(bf16[64,8,16,128]{3,1,2,0:T(8,128)(2,1)} %bitcast.53) | data formatting | bytes 4194304
  131.4 4.4 %copy.149 = bf16[512,2,8,128]{0,3,2,1:T(8,128)(2,1)} copy(bf16[512,2,8,128]{3,2,1,0:T(8,128)(2,1)} %bitcast.127) | data formatting | bytes 4194304 | tf_op jit(solution)/shard_map/while/body/eval_jaxpr/reshape | solution.py:57
  135.8 16.5 %fusion.41 = (f32[2,8,512]{2,1,0:T(8,128)S(1)}, f32[2,8,512,1024]{2,3,1,0:T(8,128)}) fusion(pred[512,1024]{0,1:T(8,128)(4,1)S(1)} %copy-done.3, bf16[512,2,8,128]{0,3,2,1:T(8,128)(2,1)S(1)} %copy.147, bf16[512,2,128]{2,0,1:T(8,128)(2,1)S(1)} %copy.134, bf16[512,2,128]{2,0,1:T(8,128)(2,1)S(1)} %copy.133), kind=kOutput, calls=%fused_computation.65 | convolution fusion | flops 4347397120 | bytes 36732928 | tf_op jit(solution)/shard_map/while/body/eval_jaxpr/sub | solution.py:66
  152.3 15.0 %fusion.20 = f32[1024,2,128]{0,2,1:T(8,128)} fusion(bf16[512,2,8,128]{0,3,2,1:T(8,128)(2,1)} %copy.149, f32[2,8,512,1024]{2,3,1,0:T(8,128)} %get-tuple-element.94, f32[2,8,512]{2,1,0:T(8,128)S(1)} %get-tuple-element.93), kind=kOutput, calls=%fused_computation.28 | convolution fusion | flops 2164260864 | bytes 36732928 | tf_op jit(solution)/shard_map/while/body/eval_jaxpr/kgrn,rkgd->nkd/dot_general | solution.py:69
  167.3 2.1 fusion.38
  169.4 1.2 copy.151
  170.6 25.4 %fusion.1 = (f32[2,8,512]{2,1,0:T(8,128)S(1)}, f32[2,1024,512,8]{2,1,3,0:T(8,128)}) fusion(f32[2,8,512,1024]{2,3,1,0:T(8,128)} %get-tuple-element.94, f32[2,8,512]{2,1,0:T(8,128)S(1)} %get-tuple-element.93, bf16[512,2,8,128]{0,3,2,1:T(8,128)(2,1)} %copy.149, bf16[512,2,128]{2,0,1:T(8,128)(2,1)} %copy.140, bf16[512,2,128]{2,0,1:T(8,128)(2,1)} %copy.139), kind=kOutput, calls=%fused_computation.3 | convolution fusion | flops 2173689856 | bytes 69795840 | tf_op jit(solution)/shard_map/while/body/eval_jaxpr/rkgd,nkd->kgrn/dot_general | solution.py:72
  196.0 27.8 %fusion.3 = bf16[2,8,512,1024]{2,3,1,0:T(8,128)(2,1)} fusion(f32[2,1024,512,8]{2,1,3,0:T(8,128)} %get-tuple-element.96, f32[2,8,512]{2,1,0:T(8,128)S(1)} %get-tuple-element.95, f32[2,8,512,1024]{2,3,1,0:T(8,128)} %get-tuple-element.94, f32[2,8,512]{2,1,0:T(8,128)S(1)} %get-tuple-element.93), kind=kLoop, calls=%fused_computation.5 | loop fusion | flops 33554432 | bytes 83951616 | tf_op jit(solution)/shard_map/while/body/eval_jaxpr/convert_element_type | solution.py:76
  223.8 9.0 %fusion.24 = f32[1024,2,128]{0,2,1:T(8,128)S(1)} fusion(bf16[2,8,512,1024]{2,3,1,0:T(8,128)(2,1)} %fusion.3, bf16[512,2,8,128]{0,3,2,1:T(8,128)(2,1)S(1)} %copy.147), kind=kOutput, calls=%fused_computation.31 | convolution fusion | flops 2147745792 | bytes 19922944 | tf_op jit(solution)/shard_map/while/body/eval_jaxpr/kgrn,rkgd->nkd/dot_general | solution.py:80
  233.1 1.0 pad_maximum_fusion
  234.2 2.1 collective-permute-start.1
  236.5 0.2 copy.152
  236.7 12.2 %collective-permute-done.1 = f32[2,512,256]{2,1,0:T(8,128)} collective-permute-done((f32[2,512,256]{2,1,0:T(8,128)}, f32[2,512,256]{2,1,0:T(8,128)}, u32[]{:S(2)}, u32[]{:S(2)}) %collective-permute-start.1) | collective-permute-done | bytes 1048608 | tf_op jit(solution)/shard_map/ppermute | solution.py:17
  248.9 1.3 fusion.37
  250.2 0.8 copy.153
  251.1 3.4 %all-to-all-start.5 = ((bf16[4,128,256]{1,2,0:T(8,128)(2,1)}), bf16[4,128,256]{1,2,0:T(8,128)(2,1)S(1)}, u32[]{:S(2)}, u32[]{:S(2)}) async-start(bf16[4,128,256]{1,2,0:T(8,128)(2,1)} %copy.153), calls=%async_computation.5 | async-start | bytes 524288 | tf_op jit(solution)/shard_map/all_to_all | solution.py:145
  255.0 0.8 copy.155
  255.8 7.2 %all-to-all-done.5 = bf16[4,128,256]{1,2,0:T(8,128)(2,1)S(1)} async-done(((bf16[4,128,256]{1,2,0:T(8,128)(2,1)}), bf16[4,128,256]{1,2,0:T(8,128)(2,1)S(1)}, u32[]{:S(2)}, u32[]{:S(2)}) %all-to-all-start.5) | async-done | bytes 262176 | tf_op jit(solution)/shard_map/all_to_all | solution.py:145
  263.1 4.1 %all-to-all-start.6 = ((bf16[4,128,256]{1,2,0:T(8,128)(2,1)}), bf16[4,128,256]{1,2,0:T(8,128)(2,1)S(1)}, u32[]{:S(2)}, u32[]{:S(2)}) async-start(bf16[4,128,256]{1,2,0:T(8,128)(2,1)} %copy.155), calls=%async_computation.6 | async-start | bytes 524288 | tf_op jit(solution)/shard_map/all_to_all | solution.py:148
  267.2 8.3 %fusion.19 = bf16[512,2,8,128]{0,3,2,1:T(8,128)(2,1)S(1)} fusion(bf16[2,8,512,1024]{2,3,1,0:T(8,128)(2,1)} %fusion.3, bf16[512,2,128]{2,0,1:T(8,128)(2,1)S(1)} %copy.134, bf16[512,2,128]{2,0,1:T(8,128)(2,1)} %copy-done.2), kind=kOutput, calls=%fused_computation.27 | convolution fusion | flops 2150629376 | bytes 19398656 | tf_op jit(solution)/shard_map/while/body/eval_jaxpr/kgrn,nkd->rkgd/dot_general | solution.py:77
  275.5 2.0 convert_element_type.43
  277.6 3.2 copy.145
  280.8 5.1 %all-to-all-start.4 = ((bf16[4,128,2048]{1,2,0:T(8,128)(2,1)}), bf16[4,128,2048]{1,2,0:T(8,128)(2,1)S(1)}, u32[]{:S(2)}, u32[]{:S(2)}) async-start(bf16[4,128,2048]{1,2,0:T(8,128)(2,1)} %copy.145), calls=%async_computation.4 | async-start | bytes 4194304 | tf_op jit(solution)/shard_map/all_to_all | solution.py:142
  285.9 0.9 copy.157
  286.7 0.9 copy.158
  287.6 47.1 %all-to-all-done.4 = bf16[4,128,2048]{1,2,0:T(8,128)(2,1)S(1)} async-done(((bf16[4,128,2048]{1,2,0:T(8,128)(2,1)}), bf16[4,128,2048]{1,2,0:T(8,128)(2,1)S(1)}, u32[]{:S(2)}, u32[]{:S(2)}) %all-to-all-start.4) | async-done | bytes 2097184 | tf_op jit(solution)/shard_map/all_to_all | solution.py:142
  334.7 2.9 copy.156
  (38 shorter events, 2.4 us)
Async XLA Ops:
  0.6 79.6 %copy-start = (s32[32,5]{0,1:T(8,128)S(1)}, s32[32,5]{0,1:T(8,128)}, u32[]{:S(2)}) copy-start(s32[32,5]{0,1:T(8,128)} %param.19) | copy-start | bytes 1924
  0.6 79.7 %copy-start.4 = (s32[8]{0:T(128)S(1)}, s32[8]{0:T(128)}, u32[]{:S(2)}) copy-start(s32[8]{0:T(128)} %param.18) | copy-start | bytes 100
  2.5 13.8 %all-to-all-start = ((bf16[128,4,256]{0,2,1:T(8,128)(2,1)}), bf16[128,4,256]{0,2,1:T(8,128)(2,1)S(1)}, u32[]{:S(2)}, u32[]{:S(2)}) async-start(bf16[128,4,256]{0,2,1:T(8,128)(2,1)} %bitcast), calls=%async_computation | async-start | bytes 524288 | tf_op jit(solution)/shard_map/all_to_all | solution.py:93
  16.2 10.4 %all-to-all-start.1 = ((bf16[128,4,256]{0,2,1:T(8,128)(2,1)}), bf16[128,4,256]{0,2,1:T(8,128)(2,1)S(1)}, u32[]{:S(2)}, u32[]{:S(2)}) async-start(bf16[128,4,256]{0,2,1:T(8,128)(2,1)} %bitcast.3), calls=%async_computation.1 | async-start | bytes 524288 | tf_op jit(solution)/shard_map/all_to_all | solution.py:94
  26.7 49.0 %all-to-all-start.2 = ((bf16[128,4,2048]{2,0,1:T(8,128)(2,1)}), bf16[128,4,2048]{2,0,1:T(8,128)(2,1)S(1)}, u32[]{:S(2)}, u32[]{:S(2)}) async-start(bf16[128,4,2048]{2,0,1:T(8,128)(2,1)} %bitcast.125), calls=%async_computation.2 | async-start | bytes 4194304 | tf_op jit(solution)/shard_map/all_to_all | solution.py:92
  75.7 52.2 %all-to-all-start.3 = ((bf16[128,4,2048]{2,0,1:T(8,128)(2,1)}), bf16[128,4,2048]{2,0,1:T(8,128)(2,1)}, u32[]{:S(2)}, u32[]{:S(2)}) async-start(bf16[128,4,2048]{2,0,1:T(8,128)(2,1)} %bitcast.123), calls=%async_computation.3 | async-start | bytes 4194304 | tf_op jit(solution)/shard_map/all_to_all | solution.py:95
  81.7 11.7 %collective-permute-start = (bf16[2,512,256]{2,1,0:T(8,128)(2,1)}, bf16[2,512,256]{2,1,0:T(8,128)(2,1)}, u32[]{:S(2)}, u32[]{:S(2)}) collective-permute-start(bf16[2,512,256]{2,1,0:T(8,128)(2,1)} %pad_maximum_fusion.1), channel_id=1, source_target_pairs={{0,4},{4,8},{8,12},{12,16},{16,20},{20,24},{24,28},{1,5},{5,9},{9,... | collective-permute-start | bytes 1572872 | tf_op jit(solution)/shard_map/ppermute | solution.py:17
  94.8 57.5 %copy-start.2 = (bf16[512,2,128]{2,0,1:T(8,128)(2,1)}, bf16[512,2,128]{2,0,1:T(8,128)(2,1)S(1)}, u32[]{:S(2)}) copy-start(bf16[512,2,128]{2,0,1:T(8,128)(2,1)S(1)} %copy.133) | copy-start | bytes 786436
  95.0 40.8 %copy-start.3 = (pred[512,1024]{0,1:T(8,128)(4,1)S(1)}, pred[512,1024]{0,1:T(8,128)(4,1)}, u32[]{:S(2)}) copy-start(pred[512,1024]{0,1:T(8,128)(4,1)} %fusion.18) | copy-start | bytes 1572868
  234.2 14.7 %collective-permute-start.1 = (f32[2,512,256]{2,1,0:T(8,128)}, f32[2,512,256]{2,1,0:T(8,128)}, u32[]{:S(2)}, u32[]{:S(2)}) collective-permute-start(f32[2,512,256]{2,1,0:T(8,128)} %pad_maximum_fusion), channel_id=1, source_target_pairs={{4,0},{8,4},{12,8},{16,12},{20,16},{24,20},{28,24},{5,1},{9,5},{13... | collective-permute-start | bytes 3145736 | tf_op jit(solution)/shard_map/ppermute | solution.py:17
  251.1 12.0 %all-to-all-start.5 = ((bf16[4,128,256]{1,2,0:T(8,128)(2,1)}), bf16[4,128,256]{1,2,0:T(8,128)(2,1)S(1)}, u32[]{:S(2)}, u32[]{:S(2)}) async-start(bf16[4,128,256]{1,2,0:T(8,128)(2,1)} %copy.153), calls=%async_computation.5 | async-start | bytes 524288 | tf_op jit(solution)/shard_map/all_to_all | solution.py:145
  263.1 17.7 %all-to-all-start.6 = ((bf16[4,128,256]{1,2,0:T(8,128)(2,1)}), bf16[4,128,256]{1,2,0:T(8,128)(2,1)S(1)}, u32[]{:S(2)}, u32[]{:S(2)}) async-start(bf16[4,128,256]{1,2,0:T(8,128)(2,1)} %copy.155), calls=%async_computation.6 | async-start | bytes 524288 | tf_op jit(solution)/shard_map/all_to_all | solution.py:148
  267.2 70.4 %copy-start.1 = (s32[32,5]{0,1:T(8,128)S(1)}, s32[32,5]{0,1:T(8,128)}, u32[]{:S(2)}) copy-start(s32[32,5]{0,1:T(8,128)} %param.19) | copy-start | bytes 1924
  280.8 53.9 %all-to-all-start.4 = ((bf16[4,128,2048]{1,2,0:T(8,128)(2,1)}), bf16[4,128,2048]{1,2,0:T(8,128)(2,1)S(1)}, u32[]{:S(2)}, u32[]{:S(2)}) async-start(bf16[4,128,2048]{1,2,0:T(8,128)(2,1)} %copy.145), calls=%async_computation.4 | async-start | bytes 4194304 | tf_op jit(solution)/shard_map/all_to_all | solution.py:142
where the time goes:
time: 339 us; the launch traced here: 338 us
  waiting for transfers between devices  154 us (45%)
  matrix products  74.2 us (22%)
  local copies, waits for them, and re-layouts  43.7 us (13%)
  starting transfers between devices  33 us (10%)
  other arithmetic  31.9 us (9%)
    all_to_all x1, waiting for transfers between devices, regrouped_body(): lax.all_to_all(query_parts.reshape(local_rows, -1), 'head', split_axis=0,...  47.1 us
    all_to_all x1, waiting for transfers between devices, regrouped_body(): lax.all_to_all(queries, 'head', split_axis=1, concat_axis=0, tiled=True)  42.3 us
    convert_element_type x1, other arithmetic, block_grads(): score_grad = (probs * (prob_grad - row_dot)).astype(jnp.bfloat16)  27.8 us
    all_to_all x1, waiting for transfers between devices, regrouped_body(): lax.all_to_all(grad_out, 'head', split_axis=1, concat_axis=0, tiled=True)  27.1 us
    dot_general x1, matrix products, block_grads(): jnp.einsum('rkgd,nkd->kgrn', grad_heads, value_heads, preferred_element_t...  25.4 us
    ppermute x2, waiting for transfers between devices, from_behind(): return lax.ppermute(value, axis, pairs)  19.2 us
    sub x1, matrix products, block_grads(): expo = jnp.exp(jnp.where(mask, score - peak, -1e+30))  16.5 us
    dot_general x1, matrix products, block_grads(): jnp.einsum('kgrn,rkgd->nkd', probs_low, grad_heads, preferred_element_typ...  15 us
  transfers between devices with their start and end apart: 9, of which 8 were waited for; matrix products, arithmetic and copies ran while one was open for 11% of the time, Pallas kernels for 0%

commit v1 on v0

v1 whole, which is shorter than its diff:
```python
import functools
import math

import jax
import jax.numpy as jnp
from jax import lax
from jax.experimental import pallas as pl
from jax.experimental.pallas import tpu as pltpu
from jax.sharding import PartitionSpec as P

KV_HEADS = 8
HEAD_DIM = 128
WINDOW = 512
BLOCK = 128
BACK = WINDOW // BLOCK
AXES = ("seq", "head")
GROUPS = 2

SCALE = 1.0 / math.sqrt(HEAD_DIM)


def mask_bias(first_row, starts_ref, pattern_ref, block):
    shape = ((BACK + 1) * BLOCK, BLOCK)
    row = lax.broadcasted_iota(jnp.int32, shape, 0)
    query_pos = first_row + lax.broadcasted_iota(jnp.int32, shape, 1)
    back = row // BLOCK
    key_pos = first_row - back * BLOCK + (row - back * BLOCK)
    crossed = jnp.zeros(shape, jnp.int32)
    for i in range(starts_ref.shape[0]):
        start = starts_ref[i]
        crossed += ((start <= query_pos) & (start > key_pos)).astype(jnp.int32)
    opened = jnp.zeros(shape, jnp.int32)
    for r in range(BACK + 1):
        opened += jnp.where(back == r, pattern_ref[block, r], 0)
    allowed = (
        (key_pos <= query_pos)
        & (query_pos - key_pos < WINDOW)
        & (key_pos >= 0)
        & (crossed == 0)
        & (opened > 0)
    )
    return jnp.where(allowed, 0.0, -1e30).astype(jnp.float32)


def dot(a, b, dims):
    return lax.dot_general(a, b, (dims, ((), ())), preferred_element_type=jnp.float32)


def head_terms(query_ref, grad_ref, query_grad_ref, first_col, group, key, value, bias):
    key_grad = None
    value_grad = None
    bias = jnp.concatenate([bias, bias], axis=1)
    for pair in range(group // 2):
        cols = [pl.ds(first_col + (2 * pair + i) * HEAD_DIM, HEAD_DIM) for i in range(2)]
        query = jnp.concatenate([query_ref[:, c] for c in cols], axis=0)
        grad = jnp.concatenate([grad_ref[:, c] for c in cols], axis=0)
        score = dot(key, query, ((1,), (1,))) * (SCALE * math.log2(math.e)) + bias
        expo = jnp.exp2(score - jnp.max(score, axis=0, keepdims=True))
        probs = expo * (1.0 / jnp.sum(expo, axis=0, keepdims=True))
        probs_low = probs.astype(jnp.bfloat16)
        prob_grad = dot(value, grad, ((1,), (1,)))
        row_dot = jnp.sum(probs * prob_grad, axis=0, keepdims=True)
        score_grad = (probs * (prob_grad - row_dot)).astype(jnp.bfloat16)
        value_part = dot(probs_low, grad, ((1,), (0,)))
        key_part = dot(score_grad, query, ((1,), (0,)))
        value_grad = value_part if value_grad is None else value_grad + value_part
        key_grad = key_part if key_grad is None else key_grad + key_part
        query_grad = (dot(score_grad, key, ((0,), (0,))) * SCALE).astype(jnp.bfloat16)
        for i in range(2):
            query_grad_ref[:, cols[i]] = query_grad[i * BLOCK : (i + 1) * BLOCK]
    return key_grad * SCALE, value_grad


def kernel(group, starts_ref, pattern_ref, query_ref, grad_ref, *refs):
    kv_refs, (query_grad_ref, own_ref, sent_ref, bias_ref) = refs[: BACK + 1], refs[BACK + 1 :]
    block = lax.axis_index("seq") * lax.axis_size("head") + lax.axis_index("head")

    @pl.when(pl.program_id(0) == 0)
    def _():
        bias_ref[...] = mask_bias(block * BLOCK, starts_ref, pattern_ref, block)

    key = jnp.concatenate([ref[0] for ref in kv_refs], axis=0)
    value = jnp.concatenate([ref[1] for ref in kv_refs], axis=0)
    key_grad, value_grad = head_terms(
        query_ref, grad_ref, query_grad_ref, 0, group, key, value, bias_ref[...]
    )
    for i, full in enumerate((key_grad, value_grad)):
        own_ref[i] = full[:BLOCK]
        for r in range(BACK):
            sent_ref[r, i] = full[(r + 1) * BLOCK : (r + 2) * BLOCK].astype(jnp.bfloat16)


def local_grads(part, heads, group, starts, pattern, queries, grad_out, kvs):
    width = group * HEAD_DIM
    wide = pl.BlockSpec((BLOCK, width), lambda h: (0, part * heads + h))
    kv_spec = pl.BlockSpec((2, BLOCK, HEAD_DIM), lambda h: (0, 0, h))
    kv_width = heads * HEAD_DIM
    smem = pl.BlockSpec(memory_space=pltpu.SMEM)
    return pl.pallas_call(
        functools.partial(kernel, group),
        grid=(heads,),
        in_specs=[smem, smem, wide, wide] + [kv_spec] * (BACK + 1),
        out_specs=[
            pl.BlockSpec((BLOCK, width), lambda h: (0, h)),
            kv_spec,
            pl.BlockSpec((BACK, 2, BLOCK, HEAD_DIM), lambda h: (0, 0, 0, h)),
        ],
        out_shape=[
            jax.ShapeDtypeStruct((BLOCK, heads * width), jnp.bfloat16),
            jax.ShapeDtypeStruct((2, BLOCK, kv_width), jnp.float32),
            jax.ShapeDtypeStruct((BACK, 2, BLOCK, kv_width), jnp.bfloat16),
        ],
        scratch_shapes=[pltpu.VMEM(((BACK + 1) * BLOCK, BLOCK), jnp.float32)],
        compiler_params=pltpu.CompilerParams(vmem_limit_bytes=40 * 2**20),
        cost_estimate=pl.CostEstimate(
            flops=heads * group * BLOCK * (BACK + 1) * BLOCK * HEAD_DIM * 40,
            bytes_accessed=heads * width * BLOCK * 6,
            transcendentals=0,
        ),
    )(starts, pattern, queries, grad_out, *kvs)


def body(queries, keys, values, grad_out, starts, pattern):
    devices = lax.axis_size("seq") * lax.axis_size("head")
    group = queries.shape[1] // keys.shape[1]
    heads = KV_HEADS // GROUPS
    kv_width = heads * HEAD_DIM
    received = []
    for part in range(GROUPS):
        cols = slice(part * kv_width, (part + 1) * kv_width)
        own = jnp.stack([keys[:, cols], values[:, cols]])
        received.append(
            [own]
            + [
                lax.ppermute(own, AXES, [(i, i + r) for i in range(devices - r)])
                for r in range(1, BACK + 1)
            ]
        )
    query_parts, kv_parts = [], []
    for part in range(GROUPS):
        query_grads, total, sent = local_grads(
            part, heads, group, starts, pattern, queries, grad_out, received[part]
        )
        query_parts.append(query_grads)
        for r in range(1, BACK + 1):
            back = lax.ppermute(sent[r - 1], AXES, [(i + r, i) for i in range(devices - r)])
            total = total + back.astype(jnp.float32)
        kv_parts.append(total.astype(jnp.bfloat16))
    both = jnp.concatenate(kv_parts, axis=2)
    return jnp.concatenate(query_parts, axis=1), both[0], both[1]


def solution(mesh):
    rows = P(AXES, None)
    return jax.shard_map(
        body,
        mesh=mesh,
        in_specs=(rows, rows, rows, rows, P(), P()),
        out_specs=(rows, rows, rows),
        check_vma=False,
    )
```

time: 339 us -> 122 us (0.36)
  waiting for transfers between devices: 154 us -> 14.5 us
  matrix products: 74.2 us -> 0 us
  local copies, waits for them, and re-layouts: 43.7 us -> 3.18 us
  starting transfers between devices: 33 us -> 69.1 us
  Pallas kernels: 0 us -> 30.9 us
  other arithmetic: 31.9 us -> 2.75 us
    all_to_all x7 -> x0, waiting for transfers between devices: 135 us -> none  [the longest x1 47.1 us: regrouped_body(): lax.all_to_all(query_parts.reshape(local_rows, -1), 'head', split_axis=0,...]
    ppermute x2 -> x16, starting transfers between devices: 4 us -> 69.1 us  [the longest x8 43.5 us: body(): lax.ppermute(own, AXES, [(i, i + r) for i in range(devices - r)])]
    dot_general x4 -> x0, matrix products: 57.7 us -> none  [the longest x1 25.4 us: block_grads(): jnp.einsum('rkgd,nkd->kgrn', grad_heads, value_heads, preferred_element_t...]
    pallas_call x0 -> x2, Pallas kernels: none -> 30.9 us  [local_grads(): pl.pallas_call(functools.partial(kernel, group), grid=(heads,), in_specs=...]
    all_to_all x7 -> x0, starting transfers between devices: 29 us -> none  [the longest x1 5.09 us: regrouped_body(): lax.all_to_all(query_parts.reshape(local_rows, -1), 'head', split_axis=0,...]
    convert_element_type x3 -> x2, other arithmetic: 28 us -> 0.37 us  [body(): kv_parts.append(total.astype(jnp.bfloat16))]
    sub x1 -> x0, matrix products: 16.5 us -> none  [block_grads(): expo = jnp.exp(jnp.where(mask, score - peak, -1e+30))]
    unnamed x17 -> x9, local copies, waits for them, and re-layouts: 13.7 us -> 1.69 us
  transfers between devices with their start and end apart: 9 -> 16, of which waited for: 8 -> 1; matrix products, arithmetic and copies ran while one was open for 11% -> 2% of each run, Pallas kernels for 0% -> 25%
where the time goes in v1:
time: 122 us; the launch traced here: 121 us
  starting transfers between devices  69.1 us (57%)
  Pallas kernels  30.9 us (25%)
  waiting for transfers between devices  14.5 us (12%)
  local copies, waits for them, and re-layouts  3.18 us (3%)
  other arithmetic  2.75 us (2%)
    ppermute x8, starting transfers between devices, body(): lax.ppermute(own, AXES, [(i, i + r) for i in range(devices - r)])  43.5 us
    pallas_call x2, Pallas kernels, local_grads(): pl.pallas_call(functools.partial(kernel, group), grid=(heads,), in_specs=...  30.9 us
    ppermute x8, starting transfers between devices, body(): lax.ppermute(sent[r - 1], AXES, [(i + r, i) for i in range(devices - r)])  25.5 us
    ppermute x8, waiting for transfers between devices, body(): lax.ppermute(sent[r - 1], AXES, [(i + r, i) for i in range(devices - r)])  14.5 us
  transfers between devices with their start and end apart: 16, of which 1 were waited for; matrix products, arithmetic and copies ran while one was open for 2% of the time, Pallas kernels for 25%

profile of v1, /device:TPU:4, one launch (start us, length us, event | category | flops | bytes accessed | tf_op | source)
XLA Modules:
  0.0 121.4 jit_solution(2156249407037937188)
XLA Ops:
  0.6 0.0 copy-start.3
  0.6 0.0 copy-start.2
  0.7 0.0 copy-start
  0.7 1.3 %slice_bitcast_fusion.10 = (bf16[1,128,512]{2,1,0:T(8,128)(2,1)S(1)}, bf16[1,128,512]{2,1,0:T(8,128)(2,1)S(1)}, bf16[1,128,512]{2,1,0:T(8,128)(2,1)S(1)}, bf16[1,128,512]{2,1,0:T(8,128)(2,1)S(1)}) fusion(bf16[128,1024]{1,0:T(8,128)(2,1)} %param.8, bf16[128,1024]{1,0:T(8,128)(2,1)} %param.7), kind=kLoop, calls=%fused_computation.21 | loop fusion | bytes 1048576 | tf_op jit(solution)/shard_map/stack | solution.py:131
  2.0 3.5 %collective-permute-start = (bf16[2,128,512]{2,1,0:T(8,128)(2,1)S(1)}, bf16[2,128,512]{2,1,0:T(8,128)(2,1)S(1)}, u32[]{:S(2)}, u32[]{:S(2)}) collective-permute-start(bf16[2,128,512]{2,1,0:T(8,128)(2,1)S(1)} %pad_maximum_fusion.2.refs_0_), channel_id=1, source_target_pairs={{0,1},{1,2},{2,3},{3,4},{4,5},{5,6},{6,7},{7,8},{8,9},{9,10},{10,1... | collective-permute-start | bytes 786440 | tf_op jit(solution)/shard_map/ppermute | solution.py:135
  5.5 4.5 %collective-permute-start.1 = (bf16[2,128,512]{2,1,0:T(8,128)(2,1)S(1)}, bf16[2,128,512]{2,1,0:T(8,128)(2,1)S(1)}, u32[]{:S(2)}, u32[]{:S(2)}) collective-permute-start(bf16[2,128,512]{2,1,0:T(8,128)(2,1)S(1)} %pad_maximum_fusion.2.refs_0_), channel_id=1, source_target_pairs={{0,2},{1,3},{2,4},{3,5},{4,6},{5,7},{6,8},{7,9},{8,10},{9,11},{10,... | collective-permute-start | bytes 786440 | tf_op jit(solution)/shard_map/ppermute | solution.py:135
  10.0 2.4 %collective-permute-start.2 = (bf16[2,128,512]{2,1,0:T(8,128)(2,1)S(1)}, bf16[2,128,512]{2,1,0:T(8,128)(2,1)}, u32[]{:S(2)}, u32[]{:S(2)}) collective-permute-start(bf16[2,128,512]{2,1,0:T(8,128)(2,1)S(1)} %pad_maximum_fusion.2.refs_0_), channel_id=1, source_target_pairs={{0,3},{1,4},{2,5},{3,6},{4,7},{5,8},{6,9},{7,10},{8,11},{9,12},{10... | collective-permute-start | bytes 786440 | tf_op jit(solution)/shard_map/ppermute | solution.py:135
  12.4 3.5 %collective-permute-start.3 = (bf16[2,128,512]{2,1,0:T(8,128)(2,1)S(1)}, bf16[2,128,512]{2,1,0:T(8,128)(2,1)}, u32[]{:S(2)}, u32[]{:S(2)}) collective-permute-start(bf16[2,128,512]{2,1,0:T(8,128)(2,1)S(1)} %pad_maximum_fusion.2.refs_0_), channel_id=1, source_target_pairs={{0,4},{1,5},{2,6},{3,7},{4,8},{5,9},{6,10},{7,11},{8,12},{9,13},{1... | collective-permute-start | bytes 786440 | tf_op jit(solution)/shard_map/ppermute | solution.py:135
  16.0 2.9 %collective-permute-start.4 = (bf16[2,128,512]{2,1,0:T(8,128)(2,1)S(1)}, bf16[2,128,512]{2,1,0:T(8,128)(2,1)S(1)}, u32[]{:S(2)}, u32[]{:S(2)}) collective-permute-start(bf16[2,128,512]{2,1,0:T(8,128)(2,1)S(1)} %pad_maximum_fusion.3.refs_0_), channel_id=1, source_target_pairs={{0,1},{1,2},{2,3},{3,4},{4,5},{5,6},{6,7},{7,8},{8,9},{9,10},{10,1... | collective-permute-start | bytes 786440 | tf_op jit(solution)/shard_map/ppermute | solution.py:135
  18.8 0.0 copy-done.3
  18.8 0.1 copy.9.pattern_ref
  18.9 0.0 collective-permute-done.refs_1_
  18.9 9.9 %collective-permute-start.5 = (bf16[2,128,512]{2,1,0:T(8,128)(2,1)S(1)}, bf16[2,128,512]{2,1,0:T(8,128)(2,1)S(1)}, u32[]{:S(2)}, u32[]{:S(2)}) collective-permute-start(bf16[2,128,512]{2,1,0:T(8,128)(2,1)S(1)} %pad_maximum_fusion.3.refs_0_), channel_id=1, source_target_pairs={{0,2},{1,3},{2,4},{3,5},{4,6},{5,7},{6,8},{7,9},{8,10},{9,11},{10,... | collective-permute-start | bytes 786440 | tf_op jit(solution)/shard_map/ppermute | solution.py:135
  28.8 0.0 collective-permute-done.1.refs_2_
  28.8 14.9 %collective-permute-start.6 = (bf16[2,128,512]{2,1,0:T(8,128)(2,1)S(1)}, bf16[2,128,512]{2,1,0:T(8,128)(2,1)S(1)}, u32[]{:S(2)}, u32[]{:S(2)}) collective-permute-start(bf16[2,128,512]{2,1,0:T(8,128)(2,1)S(1)} %pad_maximum_fusion.3.refs_0_), channel_id=1, source_target_pairs={{0,3},{1,4},{2,5},{3,6},{4,7},{5,8},{6,9},{7,10},{8,11},{9,12},{10... | collective-permute-start | bytes 786440 | tf_op jit(solution)/shard_map/ppermute | solution.py:135
  43.8 0.0 collective-permute-done.2.refs_3_
  43.8 1.9 %collective-permute-start.7 = (bf16[2,128,512]{2,1,0:T(8,128)(2,1)S(1)}, bf16[2,128,512]{2,1,0:T(8,128)(2,1)S(1)}, u32[]{:S(2)}, u32[]{:S(2)}) collective-permute-start(bf16[2,128,512]{2,1,0:T(8,128)(2,1)S(1)} %pad_maximum_fusion.3.refs_0_), channel_id=1, source_target_pairs={{0,4},{1,5},{2,6},{3,7},{4,8},{5,9},{6,10},{7,11},{8,12},{9,13},{1... | collective-permute-start | bytes 786440 | tf_op jit(solution)/shard_map/ppermute | solution.py:135
  45.7 0.0 collective-permute-done.3.refs_4_
  45.7 0.0 copy-start.1
  45.8 1.6 %copy-done.1 = bf16[128,8192]{1,0:T(8,128)(2,1)S(1)} copy-done((bf16[128,8192]{1,0:T(8,128)(2,1)S(1)}, bf16[128,8192]{1,0:T(8,128)(2,1)}, u32[]{:S(2)}) %copy-start.1) | copy-done | bytes 2097176
  47.3 15.4 %shard_map.85 = (bf16[128,4096]{1,0:T(8,128)(2,1)S(1)}, f32[2,128,512]{2,1,0:T(8,128)S(1)}, bf16[4,2,128,512]{3,2,1,0:T(8,128)(2,1)S(1)}) custom-call(s32[8]{0:T(128)S(1)} %copy-done.2, s32[32,5]{1,0:T(8,128)S(1)} %copy.9.pattern_ref, bf16[128,8192]{1,0:T(8,128)(2,1)S(1)} %copy-done, bf16[128,8192]{1,0:T(8,128)(2,1)S(1)} %copy-done.1, ...), custom_call_target="tpu_custom_call" | custom-call | flops 13421772800 | bytes 3145728 | tf_op jit(solution)/shard_map/pallas_call | solution.py:99
  62.8 0.1 slice_bitcast_fusion.7
  62.9 4.5 %collective-permute-start.10 = (bf16[2,128,512]{2,1,0:T(8,128)(2,1)S(1)}, bf16[2,128,512]{2,1,0:T(8,128)(2,1)S(1)}, u32[]{:S(2)}, u32[]{:S(2)}) collective-permute-start(bf16[2,128,512]{2,1,0:T(8,128)(2,1)S(1)} %get-tuple-element.21), channel_id=1, source_target_pairs={{3,0},{4,1},{5,2},{6,3},{7,4},{8,5},{9,6},{10,7},{11,8},{12,9},{13... | collective-permute-start | bytes 786440 | tf_op jit(solution)/shard_map/ppermute | solution.py:146
  67.4 0.0 collective-permute-done.4.refs_1_
  67.4 2.0 %collective-permute-start.11 = (bf16[2,128,512]{2,1,0:T(8,128)(2,1)S(1)}, bf16[2,128,512]{2,1,0:T(8,128)(2,1)S(1)}, u32[]{:S(2)}, u32[]{:S(2)}) collective-permute-start(bf16[2,128,512]{2,1,0:T(8,128)(2,1)S(1)} %get-tuple-element.20), channel_id=1, source_target_pairs={{4,0},{5,1},{6,2},{7,3},{8,4},{9,5},{10,6},{11,7},{12,8},{13,9},{1... | collective-permute-start | bytes 786440 | tf_op jit(solution)/shard_map/ppermute | solution.py:146
  69.4 0.0 collective-permute-done.5.refs_2_
  69.4 4.9 %collective-permute-start.8 = (bf16[2,128,512]{2,1,0:T(8,128)(2,1)S(1)}, bf16[2,128,512]{2,1,0:T(8,128)(2,1)S(1)}, u32[]{:S(2)}, u32[]{:S(2)}) collective-permute-start(bf16[2,128,512]{2,1,0:T(8,128)(2,1)S(1)} %get-tuple-element.19), channel_id=1, source_target_pairs={{1,0},{2,1},{3,2},{4,3},{5,4},{6,5},{7,6},{8,7},{9,8},{10,9},{11,1... | collective-permute-start | bytes 786440 | tf_op jit(solution)/shard_map/ppermute | solution.py:146
  74.3 0.0 collective-permute-done.6.refs_3_
  74.3 1.9 %collective-permute-start.9 = (bf16[2,128,512]{2,1,0:T(8,128)(2,1)S(1)}, bf16[2,128,512]{2,1,0:T(8,128)(2,1)S(1)}, u32[]{:S(2)}, u32[]{:S(2)}) collective-permute-start(bf16[2,128,512]{2,1,0:T(8,128)(2,1)S(1)} %get-tuple-element.22), channel_id=1, source_target_pairs={{2,0},{3,1},{4,2},{5,3},{6,4},{7,5},{8,6},{9,7},{10,8},{11,9},{12,... | collective-permute-start | bytes 786440 | tf_op jit(solution)/shard_map/ppermute | solution.py:146
  76.2 0.0 collective-permute-done.7.refs_4_
  76.2 15.5 %shard_map.86 = (bf16[128,4096]{1,0:T(8,128)(2,1)S(1)}, f32[2,128,512]{2,1,0:T(8,128)S(1)}, bf16[4,2,128,512]{3,2,1,0:T(8,128)(2,1)S(1)}) custom-call(s32[8]{0:T(128)S(1)} %copy-done.2, s32[32,5]{1,0:T(8,128)S(1)} %copy.9.pattern_ref, bf16[128,8192]{1,0:T(8,128)(2,1)S(1)} %copy-done, bf16[128,8192]{1,0:T(8,128)(2,1)S(1)} %copy-done.1, ...), custom_call_target="tpu_custom_call" | custom-call | flops 13421772800 | bytes 3145728 | tf_op jit(solution)/shard_map/pallas_call | solution.py:99
  91.7 0.1 slice_bitcast_fusion.3
  91.8 2.2 %collective-permute-start.12 = (bf16[2,128,512]{2,1,0:T(8,128)(2,1)S(1)}, bf16[2,128,512]{2,1,0:T(8,128)(2,1)S(1)}, u32[]{:S(2)}, u32[]{:S(2)}) collective-permute-start(bf16[2,128,512]{2,1,0:T(8,128)(2,1)S(1)} %get-tuple-element.15), channel_id=1, source_target_pairs={{1,0},{2,1},{3,2},{4,3},{5,4},{6,5},{7,6},{8,7},{9,8},{10,9},{11,1... | collective-permute-start | bytes 786440 | tf_op jit(solution)/shard_map/ppermute | solution.py:146
  94.0 1.5 %pad_maximum_fusion = bf16[128,8192]{1,0:T(8,128)(2,1)} fusion(bf16[128,4096]{1,0:T(8,128)(2,1)S(1)} %get-tuple-element.10, bf16[128,4096]{1,0:T(8,128)(2,1)S(1)} %get-tuple-element.9), kind=kLoop, calls=%fused_computation | loop fusion | flops 4194304 | bytes 4194304 | tf_op jit(solution)/shard_map/concatenate | solution.py:150
  95.5 0.0 collective-permute-done.10
  95.5 4.5 %collective-permute-start.13 = (bf16[2,128,512]{2,1,0:T(8,128)(2,1)S(1)}, bf16[2,128,512]{2,1,0:T(8,128)(2,1)S(1)}, u32[]{:S(2)}, u32[]{:S(2)}) collective-permute-start(bf16[2,128,512]{2,1,0:T(8,128)(2,1)S(1)} %get-tuple-element.18), channel_id=1, source_target_pairs={{2,0},{3,1},{4,2},{5,3},{6,4},{7,5},{8,6},{9,7},{10,8},{11,9},{12,... | collective-permute-start | bytes 786440 | tf_op jit(solution)/shard_map/ppermute | solution.py:146
  100.0 0.0 collective-permute-done.11
  100.0 3.7 %collective-permute-start.14 = (bf16[2,128,512]{2,1,0:T(8,128)(2,1)S(1)}, bf16[2,128,512]{2,1,0:T(8,128)(2,1)S(1)}, u32[]{:S(2)}, u32[]{:S(2)}) collective-permute-start(bf16[2,128,512]{2,1,0:T(8,128)(2,1)S(1)} %get-tuple-element.17), channel_id=1, source_target_pairs={{3,0},{4,1},{5,2},{6,3},{7,4},{8,5},{9,6},{10,7},{11,8},{12,9},{13... | collective-permute-start | bytes 786440 | tf_op jit(solution)/shard_map/ppermute | solution.py:146
  103.7 0.0 collective-permute-done.8
  103.7 1.9 %collective-permute-start.15 = (bf16[2,128,512]{2,1,0:T(8,128)(2,1)S(1)}, bf16[2,128,512]{2,1,0:T(8,128)(2,1)S(1)}, u32[]{:S(2)}, u32[]{:S(2)}) collective-permute-start(bf16[2,128,512]{2,1,0:T(8,128)(2,1)S(1)} %get-tuple-element.16), channel_id=1, source_target_pairs={{4,0},{5,1},{6,2},{7,3},{8,4},{9,5},{10,6},{11,7},{12,8},{13,9},{1... | collective-permute-start | bytes 786440 | tf_op jit(solution)/shard_map/ppermute | solution.py:146
  105.6 0.0 collective-permute-done.9
  105.6 0.2 add_convert_fusion.1
  105.8 0.0 collective-permute-done.12
  105.8 14.5 %collective-permute-done.13 = bf16[2,128,512]{2,1,0:T(8,128)(2,1)S(1)} collective-permute-done((bf16[2,128,512]{2,1,0:T(8,128)(2,1)S(1)}, bf16[2,128,512]{2,1,0:T(8,128)(2,1)S(1)}, u32[]{:S(2)}, u32[]{:S(2)}) %collective-permute-start.13) | collective-permute-done | bytes 262176 | tf_op jit(solution)/shard_map/ppermute | solution.py:146
  120.3 0.0 collective-permute-done.14
  120.3 0.0 collective-permute-done.15
  120.4 0.2 add_convert_fusion
  120.5 0.9 fusion.2
  (4 shorter events, 0.1 us)
Async XLA Ops:
  0.6 18.2 %copy-start.3 = (s32[32,5]{0,1:T(8,128)S(1)}, s32[32,5]{0,1:T(8,128)}, u32[]{:S(2)}) copy-start(s32[32,5]{0,1:T(8,128)} %param.11) | copy-start | bytes 1924
  0.6 45.1 %copy-start.2 = (s32[8]{0:T(128)S(1)}, s32[8]{0:T(128)}, u32[]{:S(2)}) copy-start(s32[8]{0:T(128)} %starts_ref.3) | copy-start | bytes 100
  0.7 45.1 %copy-start = (bf16[128,8192]{1,0:T(8,128)(2,1)S(1)}, bf16[128,8192]{1,0:T(8,128)(2,1)}, u32[]{:S(2)}) copy-start(bf16[128,8192]{1,0:T(8,128)(2,1)} %query_ref.3) | copy-start | bytes 6291460
  2.0 17.0 %collective-permute-start = (bf16[2,128,512]{2,1,0:T(8,128)(2,1)S(1)}, bf16[2,128,512]{2,1,0:T(8,128)(2,1)S(1)}, u32[]{:S(2)}, u32[]{:S(2)}) collective-permute-start(bf16[2,128,512]{2,1,0:T(8,128)(2,1)S(1)} %pad_maximum_fusion.2.refs_0_), channel_id=1, source_target_pairs={{0,1},{1,2},{2,3},{3,4},{4,5},{5,6},{6,7},{7,8},{8,9},{9,10},{10,1... | collective-permute-start | bytes 786440 | tf_op jit(solution)/shard_map/ppermute | solution.py:135
  5.5 23.4 %collective-permute-start.1 = (bf16[2,128,512]{2,1,0:T(8,128)(2,1)S(1)}, bf16[2,128,512]{2,1,0:T(8,128)(2,1)S(1)}, u32[]{:S(2)}, u32[]{:S(2)}) collective-permute-start(bf16[2,128,512]{2,1,0:T(8,128)(2,1)S(1)} %pad_maximum_fusion.2.refs_0_), channel_id=1, source_target_pairs={{0,2},{1,3},{2,4},{3,5},{4,6},{5,7},{6,8},{7,9},{8,10},{9,11},{10,... | collective-permute-start | bytes 786440 | tf_op jit(solution)/shard_map/ppermute | solution.py:135
  10.0 33.8 %collective-permute-start.2 = (bf16[2,128,512]{2,1,0:T(8,128)(2,1)S(1)}, bf16[2,128,512]{2,1,0:T(8,128)(2,1)}, u32[]{:S(2)}, u32[]{:S(2)}) collective-permute-start(bf16[2,128,512]{2,1,0:T(8,128)(2,1)S(1)} %pad_maximum_fusion.2.refs_0_), channel_id=1, source_target_pairs={{0,3},{1,4},{2,5},{3,6},{4,7},{5,8},{6,9},{7,10},{8,11},{9,12},{10... | collective-permute-start | bytes 786440 | tf_op jit(solution)/shard_map/ppermute | solution.py:135
  12.4 33.3 %collective-permute-start.3 = (bf16[2,128,512]{2,1,0:T(8,128)(2,1)S(1)}, bf16[2,128,512]{2,1,0:T(8,128)(2,1)}, u32[]{:S(2)}, u32[]{:S(2)}) collective-permute-start(bf16[2,128,512]{2,1,0:T(8,128)(2,1)S(1)} %pad_maximum_fusion.2.refs_0_), channel_id=1, source_target_pairs={{0,4},{1,5},{2,6},{3,7},{4,8},{5,9},{6,10},{7,11},{8,12},{9,13},{1... | collective-permute-start | bytes 786440 | tf_op jit(solution)/shard_map/ppermute | solution.py:135
  16.0 51.4 %collective-permute-start.4 = (bf16[2,128,512]{2,1,0:T(8,128)(2,1)S(1)}, bf16[2,128,512]{2,1,0:T(8,128)(2,1)S(1)}, u32[]{:S(2)}, u32[]{:S(2)}) collective-permute-start(bf16[2,128,512]{2,1,0:T(8,128)(2,1)S(1)} %pad_maximum_fusion.3.refs_0_), channel_id=1, source_target_pairs={{0,1},{1,2},{2,3},{3,4},{4,5},{5,6},{6,7},{7,8},{8,9},{9,10},{10,1... | collective-permute-start | bytes 786440 | tf_op jit(solution)/shard_map/ppermute | solution.py:135
  18.9 50.4 %collective-permute-start.5 = (bf16[2,128,512]{2,1,0:T(8,128)(2,1)S(1)}, bf16[2,128,512]{2,1,0:T(8,128)(2,1)S(1)}, u32[]{:S(2)}, u32[]{:S(2)}) collective-permute-start(bf16[2,128,512]{2,1,0:T(8,128)(2,1)S(1)} %pad_maximum_fusion.3.refs_0_), channel_id=1, source_target_pairs={{0,2},{1,3},{2,4},{3,5},{4,6},{5,7},{6,8},{7,9},{8,10},{9,11},{10,... | collective-permute-start | bytes 786440 | tf_op jit(solution)/shard_map/ppermute | solution.py:135
  28.8 45.4 %collective-permute-start.6 = (bf16[2,128,512]{2,1,0:T(8,128)(2,1)S(1)}, bf16[2,128,512]{2,1,0:T(8,128)(2,1)S(1)}, u32[]{:S(2)}, u32[]{:S(2)}) collective-permute-start(bf16[2,128,512]{2,1,0:T(8,128)(2,1)S(1)} %pad_maximum_fusion.3.refs_0_), channel_id=1, source_target_pairs={{0,3},{1,4},{2,5},{3,6},{4,7},{5,8},{6,9},{7,10},{8,11},{9,12},{10... | collective-permute-start | bytes 786440 | tf_op jit(solution)/shard_map/ppermute | solution.py:135
  43.8 32.4 %collective-permute-start.7 = (bf16[2,128,512]{2,1,0:T(8,128)(2,1)S(1)}, bf16[2,128,512]{2,1,0:T(8,128)(2,1)S(1)}, u32[]{:S(2)}, u32[]{:S(2)}) collective-permute-start(bf16[2,128,512]{2,1,0:T(8,128)(2,1)S(1)} %pad_maximum_fusion.3.refs_0_), channel_id=1, source_target_pairs={{0,4},{1,5},{2,6},{3,7},{4,8},{5,9},{6,10},{7,11},{8,12},{9,13},{1... | collective-permute-start | bytes 786440 | tf_op jit(solution)/shard_map/ppermute | solution.py:135
  45.7 1.6 %copy-start.1 = (bf16[128,8192]{1,0:T(8,128)(2,1)S(1)}, bf16[128,8192]{1,0:T(8,128)(2,1)}, u32[]{:S(2)}) copy-start(bf16[128,8192]{1,0:T(8,128)(2,1)} %grad_ref.3) | copy-start | bytes 6291460
  62.9 32.6 %collective-permute-start.10 = (bf16[2,128,512]{2,1,0:T(8,128)(2,1)S(1)}, bf16[2,128,512]{2,1,0:T(8,128)(2,1)S(1)}, u32[]{:S(2)}, u32[]{:S(2)}) collective-permute-start(bf16[2,128,512]{2,1,0:T(8,128)(2,1)S(1)} %get-tuple-element.21), channel_id=1, source_target_pairs={{3,0},{4,1},{5,2},{6,3},{7,4},{8,5},{9,6},{10,7},{11,8},{12,9},{13... | collective-permute-start | bytes 786440 | tf_op jit(solution)/shard_map/ppermute | solution.py:146
  67.4 32.6 %collective-permute-start.11 = (bf16[2,128,512]{2,1,0:T(8,128)(2,1)S(1)}, bf16[2,128,512]{2,1,0:T(8,128)(2,1)S(1)}, u32[]{:S(2)}, u32[]{:S(2)}) collective-permute-start(bf16[2,128,512]{2,1,0:T(8,128)(2,1)S(1)} %get-tuple-element.20), channel_id=1, source_target_pairs={{4,0},{5,1},{6,2},{7,3},{8,4},{9,5},{10,6},{11,7},{12,8},{13,9},{1... | collective-permute-start | bytes 786440 | tf_op jit(solution)/shard_map/ppermute | solution.py:146
  69.4 34.3 %collective-permute-start.8 = (bf16[2,128,512]{2,1,0:T(8,128)(2,1)S(1)}, bf16[2,128,512]{2,1,0:T(8,128)(2,1)S(1)}, u32[]{:S(2)}, u32[]{:S(2)}) collective-permute-start(bf16[2,128,512]{2,1,0:T(8,128)(2,1)S(1)} %get-tuple-element.19), channel_id=1, source_target_pairs={{1,0},{2,1},{3,2},{4,3},{5,4},{6,5},{7,6},{8,7},{9,8},{10,9},{11,1... | collective-permute-start | bytes 786440 | tf_op jit(solution)/shard_map/ppermute | solution.py:146
  74.3 31.3 %collective-permute-start.9 = (bf16[2,128,512]{2,1,0:T(8,128)(2,1)S(1)}, bf16[2,128,512]{2,1,0:T(8,128)(2,1)S(1)}, u32[]{:S(2)}, u32[]{:S(2)}) collective-permute-start(bf16[2,128,512]{2,1,0:T(8,128)(2,1)S(1)} %get-tuple-element.22), channel_id=1, source_target_pairs={{2,0},{3,1},{4,2},{5,3},{6,4},{7,5},{8,6},{9,7},{10,8},{11,9},{12,... | collective-permute-start | bytes 786440 | tf_op jit(solution)/shard_map/ppermute | solution.py:146
  91.8 14.0 %collective-permute-start.12 = (bf16[2,128,512]{2,1,0:T(8,128)(2,1)S(1)}, bf16[2,128,512]{2,1,0:T(8,128)(2,1)S(1)}, u32[]{:S(2)}, u32[]{:S(2)}) collective-permute-start(bf16[2,128,512]{2,1,0:T(8,128)(2,1)S(1)} %get-tuple-element.15), channel_id=1, source_target_pairs={{1,0},{2,1},{3,2},{4,3},{5,4},{6,5},{7,6},{8,7},{9,8},{10,9},{11,1... | collective-permute-start | bytes 786440 | tf_op jit(solution)/shard_map/ppermute | solution.py:146
  95.5 24.9 %collective-permute-start.13 = (bf16[2,128,512]{2,1,0:T(8,128)(2,1)S(1)}, bf16[2,128,512]{2,1,0:T(8,128)(2,1)S(1)}, u32[]{:S(2)}, u32[]{:S(2)}) collective-permute-start(bf16[2,128,512]{2,1,0:T(8,128)(2,1)S(1)} %get-tuple-element.18), channel_id=1, source_target_pairs={{2,0},{3,1},{4,2},{5,3},{6,4},{7,5},{8,6},{9,7},{10,8},{11,9},{12,... | collective-permute-start | bytes 786440 | tf_op jit(solution)/shard_map/ppermute | solution.py:146
  100.0 20.4 %collective-permute-start.14 = (bf16[2,128,512]{2,1,0:T(8,128)(2,1)S(1)}, bf16[2,128,512]{2,1,0:T(8,128)(2,1)S(1)}, u32[]{:S(2)}, u32[]{:S(2)}) collective-permute-start(bf16[2,128,512]{2,1,0:T(8,128)(2,1)S(1)} %get-tuple-element.17), channel_id=1, source_target_pairs={{3,0},{4,1},{5,2},{6,3},{7,4},{8,5},{9,6},{10,7},{11,8},{12,9},{13... | collective-permute-start | bytes 786440 | tf_op jit(solution)/shard_map/ppermute | solution.py:146
  103.7 16.7 %collective-permute-start.15 = (bf16[2,128,512]{2,1,0:T(8,128)(2,1)S(1)}, bf16[2,128,512]{2,1,0:T(8,128)(2,1)S(1)}, u32[]{:S(2)}, u32[]{:S(2)}) collective-permute-start(bf16[2,128,512]{2,1,0:T(8,128)(2,1)S(1)} %get-tuple-element.16), channel_id=1, source_target_pairs={{4,0},{5,1},{6,2},{7,3},{8,4},{9,5},{10,6},{11,7},{12,8},{13,9},{1... | collective-permute-start | bytes 786440 | tf_op jit(solution)/shard_map/ppermute | solution.py:146

commit v2 on v1

v2 whole, which is shorter than its diff:
```python
import functools
import math

import jax
import jax.numpy as jnp
from jax import lax
from jax.experimental import pallas as pl
from jax.experimental.pallas import tpu as pltpu
from jax.sharding import PartitionSpec as P

KV_HEADS = 8
HEAD_DIM = 128
WINDOW = 512
BLOCK = 128
BACK = WINDOW // BLOCK
AXES = ("seq", "head")

SCALE = 1.0 / math.sqrt(HEAD_DIM)


def mask_bias(first_row, starts_ref, pattern_ref, block):
    shape = ((BACK + 1) * BLOCK, BLOCK)
    row = lax.broadcasted_iota(jnp.int32, shape, 0)
    query_pos = first_row + lax.broadcasted_iota(jnp.int32, shape, 1)
    back = row // BLOCK
    key_pos = first_row - back * BLOCK + (row - back * BLOCK)
    crossed = jnp.zeros(shape, jnp.int32)
    for i in range(starts_ref.shape[0]):
        start = starts_ref[i]
        crossed += ((start <= query_pos) & (start > key_pos)).astype(jnp.int32)
    opened = jnp.zeros(shape, jnp.int32)
    for r in range(BACK + 1):
        opened += jnp.where(back == r, pattern_ref[block, r], 0)
    allowed = (
        (key_pos <= query_pos)
        & (query_pos - key_pos < WINDOW)
        & (key_pos >= 0)
        & (crossed == 0)
        & (opened > 0)
    )
    return jnp.where(allowed, 0.0, -1e30).astype(jnp.float32)


def dot(a, b, dims):
    return lax.dot_general(a, b, (dims, ((), ())), preferred_element_type=jnp.float32)


def head_terms(query_ref, grad_ref, query_grad_ref, first_col, group, key, value, bias):
    key_grad = None
    value_grad = None
    bias = jnp.concatenate([bias, bias], axis=1)
    for pair in range(group // 2):
        cols = [
            pl.ds(pl.multiple_of(first_col + (2 * pair + i) * HEAD_DIM, HEAD_DIM), HEAD_DIM)
            for i in range(2)
        ]
        query = jnp.concatenate([query_ref[:, c] for c in cols], axis=0)
        grad = jnp.concatenate([grad_ref[:, c] for c in cols], axis=0)
        score = dot(key, query, ((1,), (1,))) * (SCALE * math.log2(math.e)) + bias
        expo = jnp.exp2(score - jnp.max(score, axis=0, keepdims=True))
        probs = expo * (1.0 / jnp.sum(expo, axis=0, keepdims=True))
        probs_low = probs.astype(jnp.bfloat16)
        prob_grad = dot(value, grad, ((1,), (1,)))
        row_dot = jnp.sum(probs * prob_grad, axis=0, keepdims=True)
        score_grad = (probs * (prob_grad - row_dot)).astype(jnp.bfloat16)
        value_part = dot(probs_low, grad, ((1,), (0,)))
        key_part = dot(score_grad, query, ((1,), (0,)))
        value_grad = value_part if value_grad is None else value_grad + value_part
        key_grad = key_part if key_grad is None else key_grad + key_part
        query_grad = (dot(score_grad, key, ((0,), (0,))) * SCALE).astype(jnp.bfloat16)
        for i in range(2):
            query_grad_ref[:, cols[i]] = query_grad[i * BLOCK : (i + 1) * BLOCK]
    return key_grad * SCALE, value_grad


def kernel(
    group,
    starts_ref,
    pattern_ref,
    query_ref,
    grad_ref,
    key_ref,
    value_ref,
    query_grad_ref,
    key_grad_ref,
    value_grad_ref,
    own_kv,
    kv_in,
    own_grads,
    grads_out,
    grads_in,
    bias_ref,
    kv_send,
    kv_recv,
    grads_send,
    grads_recv,
):
    span = lax.axis_size("head")
    devices = lax.axis_size("seq") * span
    block = lax.axis_index("seq") * span + lax.axis_index("head")
    backs = range(1, BACK + 1)

    def place(other):
        return (lax.div(other, span), lax.rem(other, span))

    def has_next(r):
        return block + r < devices

    def has_prior(r):
        return block >= r

    def kv_copy(h, r):
        return pltpu.make_async_remote_copy(
            src_ref=own_kv.at[h],
            dst_ref=kv_in.at[r - 1, h],
            send_sem=kv_send.at[r - 1, h],
            recv_sem=kv_recv.at[r - 1, h],
            device_id=place(lax.rem(block + r, devices)),
            device_id_type=pl.DeviceIdType.MESH,
        )

    def grads_copy(h, r):
        return pltpu.make_async_remote_copy(
            src_ref=grads_out.at[r - 1, h],
            dst_ref=grads_in.at[r - 1, h],
            send_sem=grads_send.at[r - 1, h],
            recv_sem=grads_recv.at[r - 1, h],
            device_id=place(lax.rem(block + devices - r, devices)),
            device_id_type=pl.DeviceIdType.MESH,
        )

    barrier = pltpu.get_barrier_semaphore()
    for r in backs:
        for there, step in ((has_next(r), r), (has_prior(r), devices - r)):

            @pl.when(there)
            def _():
                pl.semaphore_signal(
                    barrier,
                    inc=1,
                    device_id=place(lax.rem(block + step, devices)),
                    device_id_type=pl.DeviceIdType.MESH,
                )

    for h in range(KV_HEADS):
        own_kv[h, 0] = key_ref[:, h * HEAD_DIM : (h + 1) * HEAD_DIM]
        own_kv[h, 1] = value_ref[:, h * HEAD_DIM : (h + 1) * HEAD_DIM]
    partners = jnp.minimum(block, BACK) + jnp.minimum(devices - 1 - block, BACK)
    pl.semaphore_wait(barrier, partners)

    @pl.loop(0, KV_HEADS)
    def _(h):
        for r in backs:

            @pl.when(has_next(r))
            def _():
                kv_copy(h, r).start()

    for r in backs:

        @pl.when(jnp.logical_not(has_prior(r)))
        def _():
            kv_in[r - 1] = jnp.zeros(kv_in.shape[1:], kv_in.dtype)

        @pl.when(jnp.logical_not(has_next(r)))
        def _():
            grads_in[r - 1] = jnp.zeros(grads_in.shape[1:], grads_in.dtype)

    bias_ref[...] = mask_bias(block * BLOCK, starts_ref, pattern_ref, block)

    @pl.loop(0, KV_HEADS)
    def _(h):
        for r in backs:

            @pl.when(has_prior(r))
            def _():
                kv_copy(h, r).wait_recv()

        key, value = (
            jnp.concatenate([own_kv[h, i]] + [kv_in[r - 1, h, i] for r in backs], axis=0)
            for i in range(2)
        )
        terms = head_terms(
            query_ref,
            grad_ref,
            query_grad_ref,
            h * (group * HEAD_DIM),
            group,
            key,
            value,
            bias_ref[...],
        )
        for i in range(2):
            own_grads[h, i] = terms[i][:BLOCK]
            for r in backs:
                grads_out[r - 1, h, i] = terms[i][r * BLOCK : (r + 1) * BLOCK].astype(
                    jnp.bfloat16
                )
        for r in backs:

            @pl.when(has_prior(r))
            def _():
                grads_copy(h, r).start()

    @pl.loop(0, KV_HEADS)
    def _(h):
        for r in backs:

            @pl.when(has_next(r))
            def _():
                grads_copy(h, r).wait_recv()

        cols = pl.ds(pl.multiple_of(h * HEAD_DIM, HEAD_DIM), HEAD_DIM)
        for i, out_ref in enumerate((key_grad_ref, value_grad_ref)):
            total = own_grads[h, i]
            for r in backs:
                total += grads_in[r - 1, h, i].astype(jnp.float32)
            out_ref[:, cols] = total.astype(jnp.bfloat16)

    @pl.loop(0, KV_HEADS)
    def _(h):
        for r in backs:

            @pl.when(has_next(r))
            def _():
                kv_copy(h, r).wait_send()

            @pl.when(has_prior(r))
            def _():
                grads_copy(h, r).wait_send()


def body(queries, keys, values, grad_out, starts, pattern):
    group = queries.shape[1] // keys.shape[1]
    smem = pl.BlockSpec(memory_space=pltpu.SMEM)
    vmem = pl.BlockSpec(memory_space=pltpu.VMEM)
    pair = (KV_HEADS, 2, BLOCK, HEAD_DIM)
    sems = pltpu.SemaphoreType.DMA((BACK, KV_HEADS))
    return pl.pallas_call(
        functools.partial(kernel, group),
        in_specs=[smem, smem] + [vmem] * 4,
        out_specs=[vmem] * 3,
        out_shape=[
            jax.ShapeDtypeStruct(queries.shape, jnp.bfloat16),
            jax.ShapeDtypeStruct(keys.shape, jnp.bfloat16),
            jax.ShapeDtypeStruct(values.shape, jnp.bfloat16),
        ],
        scratch_shapes=[
            pltpu.VMEM(pair, jnp.bfloat16),
            pltpu.VMEM((BACK,) + pair, jnp.bfloat16),
            pltpu.VMEM(pair, jnp.float32),
            pltpu.VMEM((BACK,) + pair, jnp.bfloat16),
            pltpu.VMEM((BACK,) + pair, jnp.bfloat16),
            pltpu.VMEM(((BACK + 1) * BLOCK, BLOCK), jnp.float32),
            sems,
            sems,
            sems,
            sems,
        ],
        compiler_params=pltpu.CompilerParams(
            collective_id=0, has_side_effects=True, vmem_limit_bytes=48 * 2**20
        ),
    )(starts, pattern, queries, grad_out, keys, values)


def solution(mesh):
    rows = P(AXES, None)
    return jax.shard_map(
        body,
        mesh=mesh,
        in_specs=(rows, rows, rows, rows, P(), P()),
        out_specs=(rows, rows, rows),
        check_vma=False,
    )
```

time: 122 us -> 108 us (0.89)
  starting transfers between devices: 69.1 us -> 0 us
  Pallas kernels: 30.9 us -> 98 us
  waiting for transfers between devices: 14.5 us -> 0 us
  local copies, waits for them, and re-layouts: 3.18 us -> 7.64 us
  other arithmetic: 2.75 us -> 0 us
    ppermute x16 -> x0, starting transfers between devices: 69.1 us -> none  [the longest x8 43.5 us: body(): lax.ppermute(own, AXES, [(i, i + r) for i in range(devices - r)])]
    pallas_call x2 -> x1, Pallas kernels: 30.9 us -> 98 us  [body(): pl.pallas_call(functools.partial(kernel, group), in_specs=[smem, smem] +...]
    ppermute x16 -> x0, waiting for transfers between devices: 14.5 us -> none  [the longest x8 14.5 us: body(): lax.ppermute(sent[r - 1], AXES, [(i + r, i) for i in range(devices - r)])]
    unnamed x9 -> x12, local copies, waits for them, and re-layouts: 1.69 us -> 7.64 us
    concatenate x1 -> x0, other arithmetic: 1.46 us -> none  [body(): return (jnp.concatenate(query_parts, axis=1), both[0], both[1])]
    another operation x1 -> x0, local copies, waits for them, and re-layouts: 1.28 us -> none  [body(): own = jnp.stack([keys[:, cols], values[:, cols]])]
  transfers between devices with their start and end apart: 16 -> 0, of which waited for: 1 -> 0; matrix products, arithmetic and copies ran while one was open for 2% -> 0% of each run, Pallas kernels for 25% -> 0%
where the time goes in v2:
time: 108 us; the launch traced here: 106 us
  Pallas kernels  98 us (91%)
  local copies, waits for them, and re-layouts  7.64 us (7%)
    pallas_call x1, Pallas kernels, body(): pl.pallas_call(functools.partial(kernel, group), in_specs=[smem, smem] +...  98 us
    unnamed x12, local copies, waits for them, and re-layouts  7.64 us

profile of v2, /device:TPU:4, one launch (start us, length us, event | category | flops | bytes accessed | tf_op | source)
XLA Modules:
  0.0 106.3 jit_solution(5809926082323028331)
XLA Ops:
  0.6 0.8 copy.9.pattern_ref
  1.4 0.0 copy-start
  1.4 1.6 %copy-done = bf16[128,8192]{1,0:T(8,128)(2,1)S(1)} copy-done((bf16[128,8192]{1,0:T(8,128)(2,1)S(1)}, bf16[128,8192]{1,0:T(8,128)(2,1)}, u32[]{:S(2)}) %copy-start) | copy-done | bytes 2097176
  3.0 0.0 copy-start.1
  3.0 0.9 copy-done.1
  3.9 0.0 copy-start.2
  3.9 0.9 copy-done.2
  4.9 0.0 copy-start.3
  4.9 0.7 copy-done.3
  5.5 98.0 %shard_map.85 = (bf16[128,8192]{1,0:T(8,128)(2,1)S(1)}, bf16[128,1024]{1,0:T(8,128)(2,1)S(1)}, bf16[128,1024]{1,0:T(8,128)(2,1)S(1)}) custom-call(s32[8]{0:T(128)S(1)} %copy-done.3, s32[32,5]{1,0:T(8,128)S(1)} %copy.9.pattern_ref, bf16[128,8192]{1,0:T(8,128)(2,1)S(1)} %copy-done, bf16[128,8192]{1,0:T(8,128)(2,1)} %grad_ref.1, ...), custom_call_target="tpu_custom_call" | custom-call | tf_op jit(solution)/shard_map/pallas_call | solution.py:239
  103.5 1.3 %copy.13 = bf16[128,8192]{1,0:T(8,128)(2,1)} copy(bf16[128,8192]{1,0:T(8,128)(2,1)S(1)} %get-tuple-element.6) | data formatting | bytes 4194304
  104.9 0.7 copy.14
  105.6 0.7 copy.15
Async XLA Ops:
  1.4 1.6 %copy-start = (bf16[128,8192]{1,0:T(8,128)(2,1)S(1)}, bf16[128,8192]{1,0:T(8,128)(2,1)}, u32[]{:S(2)}) copy-start(bf16[128,8192]{1,0:T(8,128)(2,1)} %query_ref.1) | copy-start | bytes 6291460
  3.0 0.9 copy-start.1
  3.9 0.9 copy-start.2
  4.9 0.7 copy-start.3

commit v3 on v2

--- a/solution.py
+++ b/solution.py
@@ -14,6 +14,7 @@
 BLOCK = 128
 BACK = WINDOW // BLOCK
 AXES = ("seq", "head")
+LEAD = 2
 
 SCALE = 1.0 / math.sqrt(HEAD_DIM)
 
@@ -92,6 +93,7 @@
     bias_ref,
     kv_send,
     kv_recv,
+    relay_send,
     grads_send,
     grads_recv,
 ):
@@ -108,6 +110,27 @@
 
     def has_prior(r):
         return block >= r
+
+    lane = lax.rem(block, BACK)
+    direct = {1: lane != 3, 2: (lane == 0) | (lane == 3), 3: lane != 0, 4: lane >= 0}
+    upward = lane == 2
+    downward = (lane == 1) & (block >= BACK)
+    relays = (
+        (upward, 1, ((2, 3), (1, 2))),
+        (downward, devices - 1, ((3, 2), (2, 1))),
+    )
+    early = {
+        1: upward,
+        2: upward | downward,
+        3: downward,
+        4: lane < 0,
+    }
+
+    def sends(r):
+        return has_next(r) & direct[r]
+
+    def waits_late(r):
+        return has_prior(r) & jnp.logical_not(early[r])
 
     def kv_copy(h, r):
         return pltpu.make_async_remote_copy(
@@ -129,6 +152,25 @@
             device_id_type=pl.DeviceIdType.MESH,
         )
 
+    def relay_copy(h, k, step, here, there):
+        return pltpu.make_async_remote_copy(
+            src_ref=kv_in.at[here - 1, h],
+            dst_ref=kv_in.at[there - 1, h],
+            send_sem=relay_send.at[k, h],
+            recv_sem=kv_recv.at[there - 1, h],
+            device_id=place(lax.rem(block + step, devices)),
+            device_id_type=pl.DeviceIdType.MESH,
+        )
+
+    def hand_on(h):
+        for active, step, moves in relays:
+
+            @pl.when(active)
+            def _():
+                for k, (here, there) in enumerate(moves):
+                    kv_copy(h, here).wait_recv()
+                    relay_copy(h, k, step, here, there).start()
+
     barrier = pltpu.get_barrier_semaphore()
     for r in backs:
         for there, step in ((has_next(r), r), (has_prior(r), devices - r)):
@@ -152,7 +194,7 @@
     def _(h):
         for r in backs:
 
-            @pl.when(has_next(r))
+            @pl.when(sends(r))
             def _():
                 kv_copy(h, r).start()
 
@@ -168,11 +210,18 @@
 
     bias_ref[...] = mask_bias(block * BLOCK, starts_ref, pattern_ref, block)
 
+    for h in range(LEAD):
+        hand_on(h)
+
     @pl.loop(0, KV_HEADS)
     def _(h):
-        for r in backs:
-
-            @pl.when(has_prior(r))
+        @pl.when(h + LEAD < KV_HEADS)
+        def _():
+            hand_on(h + LEAD)
+
+        for r in backs:
+
+            @pl.when(waits_late(r))
             def _():
                 kv_copy(h, r).wait_recv()
 
@@ -221,13 +270,20 @@
     def _(h):
         for r in backs:
 
-            @pl.when(has_next(r))
+            @pl.when(sends(r))
             def _():
                 kv_copy(h, r).wait_send()
 
             @pl.when(has_prior(r))
             def _():
                 grads_copy(h, r).wait_send()
+
+        for active, step, moves in relays:
+
+            @pl.when(active)
+            def _():
+                for k, (here, there) in enumerate(moves):
+                    relay_copy(h, k, step, here, there).wait_send()
 
 
 def body(queries, keys, values, grad_out, starts, pattern):
@@ -254,6 +310,7 @@
             pltpu.VMEM(((BACK + 1) * BLOCK, BLOCK), jnp.float32),
             sems,
             sems,
+            pltpu.SemaphoreType.DMA((2, KV_HEADS)),
             sems,
             sems,
         ],

time: 108 us -> 85.9 us (0.80); the launches traced: 106 us -> 85.6 us
  Pallas kernels: 98 us -> 77.3 us
    pallas_call x1, Pallas kernels: 98 us -> 77.3 us  [body(): pl.pallas_call(functools.partial(kernel, group), in_specs=[smem, smem] +...]
where the time goes in v3:
time: 85.9 us; the launch traced here: 85.6 us
  Pallas kernels  77.3 us (90%)
  local copies, waits for them, and re-layouts  7.64 us (9%)
    pallas_call x1, Pallas kernels, body(): pl.pallas_call(functools.partial(kernel, group), in_specs=[smem, smem] +...  77.3 us
    unnamed x12, local copies, waits for them, and re-layouts  7.64 us

profile of v3, /device:TPU:4, one launch (start us, length us, event | category | flops | bytes accessed | tf_op | source)
XLA Modules:
  0.0 85.6 jit_solution(11847765477417655371)
XLA Ops:
  0.6 0.8 copy.9.pattern_ref
  1.4 0.0 copy-start
  1.4 1.6 %copy-done = bf16[128,8192]{1,0:T(8,128)(2,1)S(1)} copy-done((bf16[128,8192]{1,0:T(8,128)(2,1)S(1)}, bf16[128,8192]{1,0:T(8,128)(2,1)}, u32[]{:S(2)}) %copy-start) | copy-done | bytes 2097176
  3.0 0.0 copy-start.1
  3.0 0.9 %copy-done.1 = bf16[128,1024]{1,0:T(8,128)(2,1)S(1)} copy-done((bf16[128,1024]{1,0:T(8,128)(2,1)S(1)}, bf16[128,1024]{1,0:T(8,128)(2,1)}, u32[]{:S(2)}) %copy-start.1) | copy-done | bytes 262168
  3.9 0.0 copy-start.2
  3.9 0.9 %copy-done.2 = bf16[128,1024]{1,0:T(8,128)(2,1)S(1)} copy-done((bf16[128,1024]{1,0:T(8,128)(2,1)S(1)}, bf16[128,1024]{1,0:T(8,128)(2,1)}, u32[]{:S(2)}) %copy-start.2) | copy-done | bytes 262168
  4.9 0.0 copy-start.3
  4.9 0.7 copy-done.3
  5.5 77.3 %shard_map.85 = (bf16[128,8192]{1,0:T(8,128)(2,1)S(1)}, bf16[128,1024]{1,0:T(8,128)(2,1)S(1)}, bf16[128,1024]{1,0:T(8,128)(2,1)S(1)}) custom-call(s32[8]{0:T(128)S(1)} %copy-done.3, s32[32,5]{1,0:T(8,128)S(1)} %copy.9.pattern_ref, bf16[128,8192]{1,0:T(8,128)(2,1)S(1)} %copy-done, bf16[128,8192]{1,0:T(8,128)(2,1)} %grad_ref.1, ...), custom_call_target="tpu_custom_call" | custom-call | tf_op jit(solution)/shard_map/pallas_call | solution.py:295
  82.9 1.3 %copy.13 = bf16[128,8192]{1,0:T(8,128)(2,1)} copy(bf16[128,8192]{1,0:T(8,128)(2,1)S(1)} %get-tuple-element.6) | data formatting | bytes 4194304
  84.2 0.7 copy.14
  84.9 0.7 copy.15
Async XLA Ops:
  1.4 1.6 %copy-start = (bf16[128,8192]{1,0:T(8,128)(2,1)S(1)}, bf16[128,8192]{1,0:T(8,128)(2,1)}, u32[]{:S(2)}) copy-start(bf16[128,8192]{1,0:T(8,128)(2,1)} %query_ref.1) | copy-start | bytes 6291460
  3.0 0.9 %copy-start.1 = (bf16[128,1024]{1,0:T(8,128)(2,1)S(1)}, bf16[128,1024]{1,0:T(8,128)(2,1)}, u32[]{:S(2)}) copy-start(bf16[128,1024]{1,0:T(8,128)(2,1)} %key_ref.1) | copy-start | bytes 786436
  3.9 0.9 %copy-start.2 = (bf16[128,1024]{1,0:T(8,128)(2,1)S(1)}, bf16[128,1024]{1,0:T(8,128)(2,1)}, u32[]{:S(2)}) copy-start(bf16[128,1024]{1,0:T(8,128)(2,1)} %value_ref.1) | copy-start | bytes 786436
  4.9 0.7 copy-start.3

commit v4 on v3

--- a/solution.py
+++ b/solution.py
@@ -90,12 +90,14 @@
     own_grads,
     grads_out,
     grads_in,
+    fold_in,
     bias_ref,
     kv_send,
     kv_recv,
     relay_send,
     grads_send,
     grads_recv,
+    fold_recv,
 ):
     span = lax.axis_size("head")
     devices = lax.axis_size("seq") * span
@@ -126,6 +128,11 @@
         4: lane < 0,
     }
 
+    top = lane == 3
+    bottom = (lane == 0) & (block >= BACK)
+    leaves = ((top, devices - 1, (3, 2)), (bottom, 1, (2, 1)))
+    leaf = {1: bottom, 2: top | bottom, 3: top, 4: lane < 0}
+
     def sends(r):
         return has_next(r) & direct[r]
 
@@ -171,6 +178,29 @@
                     kv_copy(h, here).wait_recv()
                     relay_copy(h, k, step, here, there).start()
 
+    def leaf_copy(h, k, step, here):
+        return pltpu.make_async_remote_copy(
+            src_ref=grads_out.at[here - 1, h],
+            dst_ref=fold_in.at[k, h],
+            send_sem=grads_send.at[here - 1, h],
+            recv_sem=fold_recv.at[k, h],
+            device_id=place(lax.rem(block + step, devices)),
+            device_id_type=pl.DeviceIdType.MESH,
+        )
+
+    def fold(h):
+        for active, step, moves in relays:
+
+            @pl.when(active)
+            def _():
+                for k, (here, _) in enumerate(moves):
+                    leaf_copy(h, k, step, here).wait_recv()
+                    grads_out[here - 1, h] = (
+                        grads_out[here - 1, h].astype(jnp.float32)
+                        + fold_in[k, h].astype(jnp.float32)
+                    ).astype(jnp.bfloat16)
+                    grads_copy(h, here).start()
+
     barrier = pltpu.get_barrier_semaphore()
     for r in backs:
         for there, step in ((has_next(r), r), (has_prior(r), devices - r)):
@@ -204,7 +234,7 @@
         def _():
             kv_in[r - 1] = jnp.zeros(kv_in.shape[1:], kv_in.dtype)
 
-        @pl.when(jnp.logical_not(has_next(r)))
+        @pl.when(jnp.logical_not(sends(r)))
         def _():
             grads_in[r - 1] = jnp.zeros(grads_in.shape[1:], grads_in.dtype)
 
@@ -247,15 +277,29 @@
                 )
         for r in backs:
 
-            @pl.when(has_prior(r))
+            @pl.when(waits_late(r) & jnp.logical_not(leaf[r]))
             def _():
                 grads_copy(h, r).start()
+
+        for active, step, sources in leaves:
+
+            @pl.when(active)
+            def _():
+                for k, here in enumerate(sources):
+                    leaf_copy(h, k, step, here).start()
+
+        @pl.when(h >= LEAD)
+        def _():
+            fold(h - LEAD)
+
+    for h in range(KV_HEADS - LEAD, KV_HEADS):
+        fold(h)
 
     @pl.loop(0, KV_HEADS)
     def _(h):
         for r in backs:
 
-            @pl.when(has_next(r))
+            @pl.when(sends(r))
             def _():
                 grads_copy(h, r).wait_recv()
 
@@ -307,12 +351,14 @@
             pltpu.VMEM(pair, jnp.float32),
             pltpu.VMEM((BACK,) + pair, jnp.bfloat16),
             pltpu.VMEM((BACK,) + pair, jnp.bfloat16),
+            pltpu.VMEM((2,) + pair, jnp.bfloat16),
             pltpu.VMEM(((BACK + 1) * BLOCK, BLOCK), jnp.float32),
             sems,
             sems,
             pltpu.SemaphoreType.DMA((2, KV_HEADS)),
             sems,
             sems,
+            pltpu.SemaphoreType.DMA((2, KV_HEADS)),
         ],
         compiler_params=pltpu.CompilerParams(
             collective_id=0, has_side_effects=True, vmem_limit_bytes=48 * 2**20

time: 85.9 us -> 77 us (0.90)
  Pallas kernels: 77.3 us -> 68.4 us
    pallas_call x1, Pallas kernels: 77.3 us -> 68.4 us  [body(): pl.pallas_call(functools.partial(kernel, group), in_specs=[smem, smem] +...]
where the time goes in v4:
time: 77 us; the launch traced here: 76.7 us
  Pallas kernels  68.4 us (89%)
  local copies, waits for them, and re-layouts  7.64 us (10%)
    pallas_call x1, Pallas kernels, body(): pl.pallas_call(functools.partial(kernel, group), in_specs=[smem, smem] +...  68.4 us
    unnamed x12, local copies, waits for them, and re-layouts  7.64 us

profile of v4, /device:TPU:4, one launch (start us, length us, event | category | flops | bytes accessed | tf_op | source)
XLA Modules:
  0.0 76.7 jit_solution(1108379589998749543)
XLA Ops:
  0.6 0.8 %copy.9.pattern_ref = s32[32,5]{1,0:T(8,128)S(1)} copy(s32[32,5]{0,1:T(8,128)} %param.11) | data formatting | bytes 1280 | tf_op args[5]
  1.4 0.0 copy-start
  1.4 1.6 %copy-done = bf16[128,8192]{1,0:T(8,128)(2,1)S(1)} copy-done((bf16[128,8192]{1,0:T(8,128)(2,1)S(1)}, bf16[128,8192]{1,0:T(8,128)(2,1)}, u32[]{:S(2)}) %copy-start) | copy-done | bytes 2097176
  3.0 0.0 copy-start.1
  3.0 0.9 %copy-done.1 = bf16[128,1024]{1,0:T(8,128)(2,1)S(1)} copy-done((bf16[128,1024]{1,0:T(8,128)(2,1)S(1)}, bf16[128,1024]{1,0:T(8,128)(2,1)}, u32[]{:S(2)}) %copy-start.1) | copy-done | bytes 262168
  3.9 0.0 copy-start.2
  3.9 0.9 %copy-done.2 = bf16[128,1024]{1,0:T(8,128)(2,1)S(1)} copy-done((bf16[128,1024]{1,0:T(8,128)(2,1)S(1)}, bf16[128,1024]{1,0:T(8,128)(2,1)}, u32[]{:S(2)}) %copy-start.2) | copy-done | bytes 262168
  4.9 0.0 copy-start.3
  4.9 0.7 copy-done.3
  5.5 68.4 %shard_map.85 = (bf16[128,8192]{1,0:T(8,128)(2,1)S(1)}, bf16[128,1024]{1,0:T(8,128)(2,1)S(1)}, bf16[128,1024]{1,0:T(8,128)(2,1)S(1)}) custom-call(s32[8]{0:T(128)S(1)} %copy-done.3, s32[32,5]{1,0:T(8,128)S(1)} %copy.9.pattern_ref, bf16[128,8192]{1,0:T(8,128)(2,1)S(1)} %copy-done, bf16[128,8192]{1,0:T(8,128)(2,1)} %grad_ref.1, ...), custom_call_target="tpu_custom_call" | custom-call | tf_op jit(solution)/shard_map/pallas_call | solution.py:339
  74.0 1.3 %copy.13 = bf16[128,8192]{1,0:T(8,128)(2,1)} copy(bf16[128,8192]{1,0:T(8,128)(2,1)S(1)} %get-tuple-element.6) | data formatting | bytes 4194304
  75.3 0.7 copy.14
  76.0 0.7 copy.15
Async XLA Ops:
  1.4 1.6 %copy-start = (bf16[128,8192]{1,0:T(8,128)(2,1)S(1)}, bf16[128,8192]{1,0:T(8,128)(2,1)}, u32[]{:S(2)}) copy-start(bf16[128,8192]{1,0:T(8,128)(2,1)} %query_ref.1) | copy-start | bytes 6291460
  3.0 0.9 %copy-start.1 = (bf16[128,1024]{1,0:T(8,128)(2,1)S(1)}, bf16[128,1024]{1,0:T(8,128)(2,1)}, u32[]{:S(2)}) copy-start(bf16[128,1024]{1,0:T(8,128)(2,1)} %key_ref.1) | copy-start | bytes 786436
  3.9 0.9 %copy-start.2 = (bf16[128,1024]{1,0:T(8,128)(2,1)S(1)}, bf16[128,1024]{1,0:T(8,128)(2,1)}, u32[]{:S(2)}) copy-start(bf16[128,1024]{1,0:T(8,128)(2,1)} %value_ref.1) | copy-start | bytes 786436
  4.9 0.7 copy-start.3
